TPU v7x, 32 devices: a whole 2x2x4 slice. The times are simulated.
32 devices in a mesh: gx: 8 (over z, y), gy: 4 (over x, core).
Axes of the slice: x: 2, y: 2, z: 4, core: 2. Of those that a mesh axis runs over, the one named last changes fastest.
Arguments:
- features: bfloat16 [48, 16, 64, 512], P('gy', 'gx'), may hold values from -6 to 6
- conv1_weight: bfloat16 [4608, 512], P(('gx', 'gy')), may hold values from -0.09375 to 0.09375
- conv2_weight: bfloat16 [4608, 512], P(('gx', 'gy')), may hold values from -0.09375 to 0.09375
- norm_gain: bfloat16 [512, 2], P(('gx', 'gy')), may hold values from 0.25 to 1.75
- norm_bias: bfloat16 [512, 2], P(('gx', 'gy')), may hold values from -3 to 3
- head_weight: bfloat16 [512, 40], P(('gx', 'gy')), may hold values from -0.75 to 0.75
- head_bias: bfloat16 [40], replicated, may hold values from -4 to 4
- labels: int32 [48, 40], P('gy'), may hold values 0 or 1
- heights: int32 [48], replicated, may hold values from 8 to 16, as said below
- widths: int32 [48], replicated, may hold values from 32 to 64, as said below
- picks: int32 [20], replicated, may hold values from 0 to 39
Outputs:
- pooled: float32 [48, 512], P('gy')
- features_grad: float32 [48, 16, 64, 512], P('gy', 'gx')
- conv1_grad: float32 [4608, 512], P(('gx', 'gy'))
- conv2_grad: float32 [4608, 512], P(('gx', 'gy'))
- gain_grad: float32 [512, 2], P(('gx', 'gy'))
- bias_grad: float32 [512, 2], P(('gx', 'gy'))
- head_grad: float32 [512, 40], P(('gx', 'gy'))
- head_bias_grad: float32 [40], replicated
Inputs may be any that keep to these rules, and one draw needn't show every extreme that they name: `heights`: some image has 16 valid rows. `widths`: some image has 64 valid columns.
All inputs are finite; a program needn't handle non-finite values. No bound on the sum of `labels` on one device may be relied on, other than what follows from the above.
Results may differ from a plain program's by a relative error of at most 0.0085.
Values may be sent and summed in bfloat16 or wider, within the bound.
A program may use at most 192 MiB of HBM per device.

v0:
```python
import jax
import jax.numpy as jnp
from jax import lax
from jax.sharding import PartitionSpec as P

TASKS = 40
MICRO = 2
STEPS = 20


norm_eps = 1e-05


def extended(cells, sides, width):
    for axis, dim in sides:
        count = lax.axis_size(axis)
        ends = count - 1
        head = lax.slice_in_dim(cells, 0, width, axis=dim)
        tail = lax.slice_in_dim(cells, cells.shape[dim] - width, cells.shape[dim], axis=dim)
        cells = jnp.concatenate(
            [
                lax.ppermute(tail, axis, [(i, (i + 1) % count) for i in range(ends)]),
                cells,
                lax.ppermute(head, axis, [((i + 1) % count, i) for i in range(ends)]),
            ],
            axis=dim,
        )
    return cells


def make_patches(padded, row_count, col_count):
    widened = jnp.pad(padded, ((0, 0), (0, 0), (1, 1), (0, 0)))
    pieces = [
        widened[:, row_off : row_off + row_count, col_off : col_off + col_count, :]
        for row_off in range(3)
        for col_off in range(3)
    ]
    joined = jnp.concatenate(pieces, axis=-1)
    return joined.reshape(-1, joined.shape[-1])


def conv_rows(act, weight):
    padded = extended(act, (("gx", 1),), 1)
    patches = make_patches(padded, act.shape[1], act.shape[2])
    output = jnp.dot(patches, weight, preferred_element_type=jnp.float32)
    return (output.reshape(act.shape[:3] + (weight.shape[1],)), padded)


def reversed_taps(weight):
    channels = weight.shape[1]
    taps = weight.reshape(9, channels, channels)[::-1]
    return jnp.transpose(taps, (0, 2, 1)).reshape(9 * channels, channels)


def weight_term(padded, grad_bf):
    patches = make_patches(padded, grad_bf.shape[1], grad_bf.shape[2])
    flat_grad = grad_bf.reshape(-1, grad_bf.shape[-1])
    return lax.dot_general(
        patches, flat_grad, (((0,), (0,)), ((), ())), preferred_element_type=jnp.float32
    )


def batch_statistics(values, inner_result, pixel_total):
    center_val = (
        lax.psum(jnp.sum(values * inner_result, axis=(0, 1, 2)), ("gx", "gy")) / pixel_total
    )
    centered = values - center_val
    spread_sq = (
        lax.psum(jnp.sum(inner_result * centered * centered, axis=(0, 1, 2)), ("gx", "gy"))
        / pixel_total
    )
    inverse_scale = lax.rsqrt(spread_sq + norm_eps)
    return (centered * inverse_scale, inverse_scale)


def norm_backward(
    output_gradient, normalized_input, inverse_scale, norm_scale_factor, inner_result, pixel_total
):
    bias_gradient_total, scale_gradient_total = lax.psum(
        (
            jnp.sum(output_gradient, axis=(0, 1, 2)),
            jnp.sum(output_gradient * normalized_input, axis=(0, 1, 2)),
        ),
        ("gx", "gy"),
    )
    backward_result = (
        norm_scale_factor
        * inverse_scale
        * (
            output_gradient
            - bias_gradient_total / pixel_total
            - normalized_input * scale_gradient_total / pixel_total
        )
        * inner_result
    )
    return (backward_result, scale_gradient_total, bias_gradient_total)


def silu_slope(values):
    sig_val = jax.nn.sigmoid(values)
    return sig_val * (1.0 + values * (1.0 - sig_val))


def frank_wolfe(gram, picks):
    task_ids = jnp.arange(TASKS)

    def fw_step(index, task_mix):
        onehot = (task_ids == picks[index]).astype(jnp.float32)
        mixed_vec = jnp.dot(gram, task_mix, precision=lax.Precision.HIGHEST)
        self_dot = jnp.sum(task_mix * mixed_vec)
        cross_dot = jnp.sum(onehot * mixed_vec)
        vertex_dot = jnp.sum(onehot * jnp.dot(gram, onehot, precision=lax.Precision.HIGHEST))
        distance = jnp.maximum(self_dot + vertex_dot - 2.0 * cross_dot, 0.1 * vertex_dot)
        step_size = jnp.clip((self_dot - cross_dot) / distance, 0.0, 1.0)
        return (1.0 - step_size) * task_mix + step_size * onehot

    start = jnp.full((TASKS,), 1.0 / TASKS, jnp.float32)
    return lax.fori_loop(0, STEPS, fw_step, start)


def on_device(
    features,
    conv1_weight,
    conv2_weight,
    norm_gain,
    norm_bias,
    head_weight,
    head_bias,
    labels,
    heights,
    widths,
    picks,
):
    image_count, row_count, col_count, channels = features.shape
    per_micro = image_count // MICRO
    total_images = image_count * lax.axis_size("gy")
    row_ids = lax.axis_index("gx") * row_count + jnp.arange(row_count)
    my_heights = lax.dynamic_slice_in_dim(heights, lax.axis_index("gy") * image_count, image_count)
    my_widths = lax.dynamic_slice_in_dim(widths, lax.axis_index("gy") * image_count, image_count)
    inside_all = (
        (row_ids[None, :, None] < my_heights[:, None, None])
        & (jnp.arange(col_count)[None, None, :] < my_widths[:, None, None])
    ).astype(jnp.float32)[..., None]
    pixel_count = (my_heights * my_widths).astype(jnp.float32)
    micro_pixels = jnp.sum((heights * widths).reshape(-1, MICRO, per_micro), axis=(0, 2)).astype(
        jnp.float32
    )

    def weights_now():
        return (
            lax.all_gather(conv1_weight, ("gx", "gy"), axis=0, tiled=True),
            lax.all_gather(conv2_weight, ("gx", "gy"), axis=0, tiled=True),
            lax.all_gather(norm_gain, ("gx", "gy"), axis=0, tiled=True),
            lax.all_gather(norm_bias, ("gx", "gy"), axis=0, tiled=True),
            lax.all_gather(head_weight, ("gx", "gy"), axis=0, tiled=True),
        )

    saved = []
    pooled_parts = []
    head_full = None
    for index in range(MICRO):
        conv_one, conv_two, gain_full, bias_full, head_full = weights_now()
        scale_factors = gain_full.astype(jnp.float32)
        bias_values = bias_full.astype(jnp.float32)
        inner_result = inside_all[index * per_micro : (index + 1) * per_micro]
        pixel_total = micro_pixels[index]
        base_input_bfloat = features[
            index * per_micro : (index + 1) * per_micro
        ] * inner_result.astype(jnp.bfloat16)
        first_convolution, padded_input = conv_rows(base_input_bfloat, conv_one)
        first_normalized, first_scale = batch_statistics(
            first_convolution, inner_result, pixel_total
        )
        first_norm_output = scale_factors[:, 0] * first_normalized + bias_values[:, 0]
        hidden_bf = (jax.nn.silu(first_norm_output) * inner_result).astype(jnp.bfloat16)
        second_convolution, padded_hidden_state = conv_rows(hidden_bf, conv_two)
        second_normalized, second_scale = batch_statistics(
            second_convolution, inner_result, pixel_total
        )
        before_activation = (
            scale_factors[:, 1] * second_normalized
            + bias_values[:, 1]
            + base_input_bfloat.astype(jnp.float32)
        )
        final_act = jax.nn.silu(before_activation) * inner_result
        pooled_parts.append(jnp.sum(final_act, axis=(1, 2)))
        saved.append(
            (
                padded_input,
                padded_hidden_state,
                first_normalized,
                first_scale,
                first_norm_output,
                second_normalized,
                second_scale,
                before_activation,
            )
        )
    pooled = lax.psum(jnp.concatenate(pooled_parts, axis=0), "gx") / pixel_count[:, None]
    head_mat = head_full.astype(jnp.float32)
    logits = jnp.dot(pooled, head_mat, precision=lax.Precision.HIGHEST) + head_bias.astype(
        jnp.float32
    )
    residual = (jax.nn.sigmoid(logits) - labels.astype(jnp.float32)) / total_images
    gram_part = jnp.dot(residual.T, residual, precision=lax.Precision.HIGHEST)
    head_part = jnp.dot(pooled.T, residual, precision=lax.Precision.HIGHEST)
    gram_sum, head_bias_grad, head_total = (
        lax.psum(gram_part.astype(jnp.bfloat16), "gy").astype(jnp.float32),
        lax.psum(jnp.sum(residual, axis=0).astype(jnp.bfloat16), "gy").astype(jnp.float32),
        lax.psum(head_part.astype(jnp.bfloat16), "gy").astype(jnp.float32),
    )
    gram = gram_sum * jnp.dot(head_mat.T, head_mat, precision=lax.Precision.HIGHEST)
    task_mix = frank_wolfe(gram, picks)
    pooled_cot = jnp.dot(residual * task_mix, head_mat.T, precision=lax.Precision.HIGHEST)
    shard_rows = 9 * channels // lax.axis_size(("gx", "gy"))
    conv1_grad = jnp.zeros((shard_rows, channels), jnp.float32)
    conv2_grad = jnp.zeros((shard_rows, channels), jnp.float32)
    gain_total = jnp.zeros((channels, 2), jnp.float32)
    bias_total = jnp.zeros((channels, 2), jnp.float32)
    feat_parts = []
    for index in range(MICRO):
        conv_one, conv_two, gain_full, bias_full, unused_heads = weights_now()
        scale_factors = gain_full.astype(jnp.float32)
        (
            padded_input,
            padded_hidden_state,
            first_normalized,
            first_scale,
            first_norm_output,
            second_normalized,
            second_scale,
            before_activation,
        ) = saved[index]
        inner_result = inside_all[index * per_micro : (index + 1) * per_micro]
        pixel_total = micro_pixels[index]
        cot_part = (
            pooled_cot[index * per_micro : (index + 1) * per_micro]
            / pixel_count[index * per_micro : (index + 1) * per_micro, None]
        )
        gradient_before_relu = (
            cot_part[:, None, None, :] * inner_result * silu_slope(before_activation)
        )
        d_second, gain_two, bias_two = norm_backward(
            gradient_before_relu,
            second_normalized,
            second_scale,
            scale_factors[:, 1],
            inner_result,
            pixel_total,
        )
        second_bf = d_second.astype(jnp.bfloat16)
        term_two = weight_term(padded_hidden_state, second_bf)
        d_hidden, unused_pad = conv_rows(second_bf, reversed_taps(conv_two))
        gradient_norm_first = d_hidden * inner_result * silu_slope(first_norm_output)
        d_first, gain_one, bias_one = norm_backward(
            gradient_norm_first,
            first_normalized,
            first_scale,
            scale_factors[:, 0],
            inner_result,
            pixel_total,
        )
        first_bf = d_first.astype(jnp.bfloat16)
        term_one = weight_term(padded_input, first_bf)
        d_base, unused_pad_two = conv_rows(first_bf, reversed_taps(conv_one))
        feat_parts.append((d_base + gradient_before_relu) * inner_result)
        gain_total = gain_total + jnp.stack([gain_one, gain_two], axis=1)
        bias_total = bias_total + jnp.stack([bias_one, bias_two], axis=1)
        shard_one, shard_two = (
            lax.psum_scatter(term_one, ("gx", "gy"), scatter_dimension=0, tiled=True),
            lax.psum_scatter(term_two, ("gx", "gy"), scatter_dimension=0, tiled=True),
        )
        conv1_grad = conv1_grad + shard_one
        conv2_grad = conv2_grad + shard_two
    flat_index = lax.axis_index(("gx", "gy"))
    chan_rows = channels // lax.axis_size(("gx", "gy"))
    gain_grad = lax.dynamic_slice_in_dim(gain_total, flat_index * chan_rows, chan_rows, 0)
    bias_grad = lax.dynamic_slice_in_dim(bias_total, flat_index * chan_rows, chan_rows, 0)
    head_grad = lax.dynamic_slice_in_dim(head_total, flat_index * chan_rows, chan_rows, 0)
    features_grad = jnp.concatenate(feat_parts, axis=0)
    return (
        pooled,
        features_grad,
        conv1_grad,
        conv2_grad,
        gain_grad,
        bias_grad,
        head_grad,
        head_bias_grad,
    )


def solution(mesh):
    in_specs = (
        P("gy", "gx", None, None),
        P(("gx", "gy"), None),
        P(("gx", "gy"), None),
        P(("gx", "gy"), None),
        P(("gx", "gy"), None),
        P(("gx", "gy"), None),
        P(),
        P("gy", None),
        P(),
        P(),
        P(),
    )
    out_specs = (
        P("gy", None),
        P("gy", "gx", None, None),
        P(("gx", "gy"), None),
        P(("gx", "gy"), None),
        P(("gx", "gy"), None),
        P(("gx", "gy"), None),
        P(("gx", "gy"), None),
        P(),
    )
    return jax.shard_map(
        on_device, mesh=mesh, in_specs=in_specs, out_specs=out_specs, check_vma=False
    )
```

profile of v0, /device:TPU:24, one launch (start us, length us, event | category | flops | bytes accessed | tf_op | source)
XLA Modules:
  0.0 979.1 jit_solution(15210543604669097085)
XLA Ops:
  27.0 37.1 %all-gather = bf16[32,16,2]{1,2,0:T(2,128)(2,1)S(1)} all-gather(bf16[1,16,2]{1,2,0:T(2,128)(2,1)S(1)} %bitcast.167), channel_id=1, replica_groups=mesh['gx'=8,'gy'=4] {'gx','gy'}, dimensions={0}, use_global_device_ids=true | all-gather | bytes 2112 | tf_op jit(solution)/shard_map/all_gather | solution.py:153
  64.2 31.7 %all-gather.1 = bf16[32,16,2]{1,2,0:T(2,128)(2,1)S(1)} all-gather(bf16[1,16,2]{1,2,0:T(2,128)(2,1)S(1)} %bitcast.168), channel_id=1, replica_groups=mesh['gx'=8,'gy'=4] {'gx','gy'}, dimensions={0}, use_global_device_ids=true | all-gather | bytes 2112 | tf_op jit(solution)/shard_map/all_gather | solution.py:154
  96.4 37.7 %all_gather.14 = bf16[512,40]{1,0:T(8,128)(2,1)S(1)} all-gather(bf16[16,40]{1,0:T(8,128)(2,1)S(1)} %copy-done.43), channel_id=1, replica_groups=mesh['gx'=8,'gy'=4] {'gx','gy'}, dimensions={0}, use_global_device_ids=true | all-gather | bytes 42240 | tf_op jit(solution)/shard_map/all_gather | solution.py:155
  149.9 9.8 multiply_reduce_fusion.7
  159.7 6.0 multiply_reduce_fusion.10
  165.7 43.8 %all-reduce.13 = (f32[512]{0:T(512)S(1)}, f32[512]{0:T(512)S(1)}) all-reduce(f32[512]{0:T(512)S(1)} %get-tuple-element.213, f32[512]{0:T(512)S(1)} %get-tuple-element.215), channel_id=1, replica_groups=mesh['gx'=8,'gy'=4] {'gx','gy'}, use_global_device_ids=true, to_apply=%region_1.2 | all-reduce | flops 1024 | bytes 8192 | tf_op jit(solution)/shard_map/psum | solution.py:65
  212.7 41.0 %all-reduce.12 = (f32[512]{0:T(512)S(1)}, f32[512]{0:T(512)S(1)}) all-reduce(f32[512]{0:T(512)S(1)} %get-tuple-element.225, f32[512]{0:T(512)S(1)} %get-tuple-element.226), channel_id=1, replica_groups=mesh['gx'=8,'gy'=4] {'gx','gy'}, use_global_device_ids=true, to_apply=%region_4.5 | all-reduce | flops 1024 | bytes 8192 | tf_op jit(solution)/shard_map/psum | solution.py:69
  266.5 4.8 reverse_bitcast_fusion.1
  271.2 6.7 copy.33
  290.4 8.3 collective-permute-done.3
  305.8 5.0 multiply_reduce_fusion.9
  310.8 38.9 %all-reduce.11 = (f32[512]{0:T(512)S(1)}, f32[512]{0:T(512)S(1)}) all-reduce(f32[512]{0:T(512)S(1)} %get-tuple-element.217, f32[512]{0:T(512)S(1)} %get-tuple-element.219), channel_id=1, replica_groups=mesh['gx'=8,'gy'=4] {'gx','gy'}, use_global_device_ids=true, to_apply=%region_6.7 | all-reduce | flops 1024 | bytes 8192 | tf_op jit(solution)/shard_map/psum | solution.py:65
  351.7 41.4 %all-reduce.10 = (f32[512]{0:T(512)S(1)}, f32[512]{0:T(512)S(1)}) all-reduce(f32[512]{0:T(512)S(1)} %fusion.26, f32[512]{0:T(512)S(1)} %fusion.28), channel_id=1, replica_groups=mesh['gx'=8,'gy'=4] {'gx','gy'}, use_global_device_ids=true, to_apply=%region_8.9 | all-reduce | flops 1024 | bytes 8192 | tf_op jit(solution)/shard_map/psum | solution.py:69
  397.6 33.3 %psum.148 = f32[12,512]{1,0:T(8,128)S(1)} all-reduce(f32[12,512]{1,0:T(8,128)S(1)} %pad_maximum_fusion.17), channel_id=1, replica_groups=mesh['gx'=8,'gy'=4] {'gx'}, use_global_device_ids=true, to_apply=%region_19.20 | all-reduce | flops 6144 | bytes 49152 | tf_op jit(solution)/shard_map/psum | solution.py:199
  432.0 12.4 %all-reduce.14 = (bf16[40,40]{1,0:T(8,128)(2,1)S(1)}, bf16[512,40]{1,0:T(8,128)(2,1)}, bf16[40]{0:T(256)(128)(2,1)}) all-reduce(bf16[40,40]{1,0:T(8,128)(2,1)S(1)} %convolution_convert_fusion.1, bf16[512,40]{1,0:T(8,128)(2,1)S(1)} %convolution_convert_fusion, ...), channel_id=1, replica_groups=mesh['gx'=8,'gy'=4] {'gy'}, use_global_device_ids=true, to_apply=%region_20.21 | all-reduce | flops 22120 | bytes 88480 | tf_op jit(solution)/shard_map/psum | solution.py:208
  444.6 159.3 %while.14 = (s32[]{:T(128)}, f32[40]{0:T(128)S(1)}, f32[40,40]{1,0:T(8,128)S(1)}, s32[20]{0:T(128)S(1)}, s32[]{:T(128)}, /*index=5*/f32[]{:T(128)}, f32[]{:T(128)}, s32[]{:T(128)}, f32[]{:T(128)}, f32[]{:T(128)}) while((s32[]{:T(128)}, f32[40]{0:T(128)S(1)}, f32[40,40]{1,0:T(8,128)S(1)}, s32[20]{0:T(128)S(1)}, s32[]{:T(128)}, ...), condition=%wide.region_25.26_spmd.clone, body=%wide.region_21.25_spmd.clone.sunk | while | flops 39050 | bytes 13564 | solution.py:118
  609.3 40.5 %all-reduce.9 = (f32[512]{0:T(512)}, f32[512]{0:T(512)S(1)}, f32[512]{0:T(512)S(1)}, f32[512]{0:T(512)S(1)}) all-reduce(f32[512]{0:T(512)S(1)} %get-tuple-element.196, f32[512]{0:T(512)S(1)} %get-tuple-element.197, f32[512]{0:T(512)S(1)} %get-tuple-element.125, ...), channel_id=1, replica_groups=mesh['gx'=8,'gy'=4] {'gx','gy'}, use_global_device_ids=true, to_apply=%region_37.38 | all-reduce | flops 2048 | bytes 16384 | tf_op jit(solution)/shard_map/psum | solution.py:79
  654.4 7.1 fusion.88
  662.2 4.4 collective-permute-start.8
  678.2 6.5 bitcast_add_fusion
  685.0 7.5 collective-permute-done.9
  695.9 4.9 collective-permute-done.13
  705.2 5.6 fusion.65
  710.8 5.6 fusion.67
  716.4 41.9 %all-reduce.8 = (f32[512]{0:T(512)S(1)}, f32[512]{0:T(512)S(1)}, f32[512]{0:T(512)S(1)}, f32[512]{0:T(512)S(1)}) all-reduce(f32[512]{0:T(512)S(1)} %get-tuple-element.127, f32[512]{0:T(512)S(1)} %get-tuple-element.126, f32[512]{0:T(512)S(1)} %get-tuple-element.123, ...), channel_id=1, replica_groups=mesh['gx'=8,'gy'=4] {'gx','gy'}, use_global_device_ids=true, to_apply=%region_41.42 | all-reduce | flops 2048 | bytes 16384 | tf_op jit(solution)/shard_map/psum | solution.py:79
  764.5 6.4 fusion.87
  771.0 6.5 bitcast_add_fusion.1
  777.5 4.8 reverse_bitcast_fusion
  782.3 6.8 copy.34
  808.8 17.8 %collective-permute-done.11 = bf16[6,1,64,512]{3,2,1,0:T(8,128)(2,1)S(1)} collective-permute-done((bf16[6,1,64,512]{3,2,1,0:T(8,128)(2,1)S(1)}, bf16[6,1,64,512]{3,2,1,0:T(8,128)(2,1)S(1)}, u32[]{:S(2)}, u32[]{:S(2)}) %collective-permute-start.11) | collective-permute-done | bytes 393248 | tf_op jit(solution)/shard_map/ppermute | solution.py:24
  828.0 4.7 collective-permute-done.15
  846.6 125.5 %reduce-scatter.3.cloned.1.call-done = f32[144,512]{1,0:T(8,128)} async-done(((f32[4608,512]{1,0:T(8,128)}), f32[144,512]{1,0:T(8,128)}) %reduce-scatter.3.cloned.1.call-update) | async-done | bytes 294928 | tf_op jit(solution)/shard_map/reduce_scatter | solution.py:270
  (393 shorter events, 227.9 us)
Async XLA Ops:
  7.2 142.7 %all-gather.5.cloned.1.call-start = ((), (), s32[]{:S(2)}) async-start(), calls=%async_computation.2 | async-start | bytes 4866048 | tf_op jit(solution)/shard_map/all_gather | solution.py:151
  7.9 258.6 %all-gather.7.cloned.1.call-start = ((), (), s32[]{:S(2)}) async-start(), calls=%async_computation.3 | async-start | bytes 4866048 | tf_op jit(solution)/shard_map/all_gather | solution.py:152
  10.7 53.5 %copy-start.45 = (bf16[16,2]{0,1:T(2,128)(2,1)S(1)}, bf16[16,2]{0,1:T(2,128)(2,1)}, u32[]{:S(2)}) copy-start(bf16[16,2]{0,1:T(2,128)(2,1)} %param.17) | copy-start | bytes 196
  10.7 85.7 %copy-start.43 = (bf16[16,40]{1,0:T(8,128)(2,1)S(1)}, bf16[16,40]{1,0:T(8,128)(2,1)}, u32[]{:S(2)}) copy-start(bf16[16,40]{1,0:T(8,128)(2,1)} %param.18) | copy-start | bytes 3844
  11.6 123.1 %collective-permute-start.4 = (bf16[6,1,64,512]{3,2,1,0:T(8,128)(2,1)}, bf16[6,1,64,512]{3,2,1,0:T(8,128)(2,1)S(1)}, u32[]{:S(2)}, u32[]{:S(2)}) collective-permute-start(bf16[6,1,64,512]{3,2,1,0:T(8,128)(2,1)} %get-tuple-element.186), channel_id=1, source_target_pairs={{0,4},{4,8},{8,12},{12,16},{16,20},{20,24},{24,28},{1,5},{5,9},{9,... | collective-permute-start | bytes 1179656 | tf_op jit(solution)/shard_map/ppermute | solution.py:22
  15.1 119.7 %collective-permute-start.5 = (bf16[6,1,64,512]{3,2,1,0:T(8,128)(2,1)}, bf16[6,1,64,512]{3,2,1,0:T(8,128)(2,1)S(1)}, u32[]{:S(2)}, u32[]{:S(2)}) collective-permute-start(bf16[6,1,64,512]{3,2,1,0:T(8,128)(2,1)} %get-tuple-element.187), channel_id=1, source_target_pairs={{4,0},{8,4},{12,8},{16,12},{20,16},{24,20},{28,24},{5,1},{9,5},{13... | collective-permute-start | bytes 1179656 | tf_op jit(solution)/shard_map/ppermute | solution.py:24
  19.3 116.8 %collective-permute-start = (bf16[6,1,64,512]{3,2,1,0:T(8,128)(2,1)}, bf16[6,1,64,512]{3,2,1,0:T(8,128)(2,1)S(1)}, u32[]{:S(2)}, u32[]{:S(2)}) collective-permute-start(bf16[6,1,64,512]{3,2,1,0:T(8,128)(2,1)} %get-tuple-element.188), channel_id=1, source_target_pairs={{0,4},{4,8},{8,12},{12,16},{16,20},{20,24},{24,28},{1,5},{5,9},{9,... | collective-permute-start | bytes 1179656 | tf_op jit(solution)/shard_map/ppermute | solution.py:22
  21.9 114.3 %collective-permute-start.1 = (bf16[6,1,64,512]{3,2,1,0:T(8,128)(2,1)}, bf16[6,1,64,512]{3,2,1,0:T(8,128)(2,1)S(1)}, u32[]{:S(2)}, u32[]{:S(2)}) collective-permute-start(bf16[6,1,64,512]{3,2,1,0:T(8,128)(2,1)} %get-tuple-element.189), channel_id=1, source_target_pairs={{4,0},{8,4},{12,8},{16,12},{20,16},{24,20},{28,24},{5,1},{9,5},{13... | collective-permute-start | bytes 1179656 | tf_op jit(solution)/shard_map/ppermute | solution.py:24
  26.1 820.5 %reduce-scatter.5.cloned.1.call-start = ((), (), s32[]{:S(2)}) async-start(), calls=%async_computation.5 | async-start | bytes 9732096 | tf_op jit(solution)/shard_map/reduce_scatter | solution.py:271
  96.2 159.5 %copy-start.36 = (f32[512,1]{0,1:T(1,128)}, f32[512,1]{0,1:T(1,128)S(1)}, u32[]{:S(2)}) copy-start(f32[512,1]{0,1:T(1,128)S(1)} %get-tuple-element.203) | copy-start | bytes 6148
  96.2 298.7 %copy-start.27 = (f32[512,1]{0,1:T(1,128)}, f32[512,1]{0,1:T(1,128)S(1)}, u32[]{:S(2)}) copy-start(f32[512,1]{0,1:T(1,128)S(1)} %get-tuple-element.204) | copy-start | bytes 6148
  96.4 159.2 %copy-start.25 = (f32[512,1]{0,1:T(1,128)}, f32[512,1]{0,1:T(1,128)S(1)}, u32[]{:S(2)}) copy-start(f32[512,1]{0,1:T(1,128)S(1)} %get-tuple-element.201) | copy-start | bytes 6148
  165.7 89.9 %copy-start.1 = (f32[6,2,64,512]{3,2,1,0:T(8,128)}, f32[6,2,64,512]{3,2,1,0:T(8,128)S(1)}, u32[]{:S(2)}) copy-start(f32[6,2,64,512]{3,2,1,0:T(8,128)S(1)} %get-tuple-element.214) | copy-start | bytes 4718596
  259.7 25.1 %collective-permute-start.6 = (bf16[6,1,64,512]{3,2,1,0:T(8,128)(2,1)}, bf16[6,1,64,512]{3,2,1,0:T(8,128)(2,1)}, u32[]{:S(2)}, u32[]{:S(2)}) collective-permute-start(bf16[6,1,64,512]{3,2,1,0:T(8,128)(2,1)} %get-tuple-element.182), channel_id=1, source_target_pairs={{0,4},{4,8},{8,12},{12,16},{16,20},{20,24},{24,28},{1,5},{5,9},{9,... | collective-permute-start | bytes 1179656 | tf_op jit(solution)/shard_map/ppermute | solution.py:22
  263.9 20.9 %collective-permute-start.7 = (bf16[6,1,64,512]{3,2,1,0:T(8,128)(2,1)}, bf16[6,1,64,512]{3,2,1,0:T(8,128)(2,1)}, u32[]{:S(2)}, u32[]{:S(2)}) collective-permute-start(bf16[6,1,64,512]{3,2,1,0:T(8,128)(2,1)} %get-tuple-element.183), channel_id=1, source_target_pairs={{4,0},{8,4},{12,8},{16,12},{20,16},{24,20},{28,24},{5,1},{9,5},{13... | collective-permute-start | bytes 1179656 | tf_op jit(solution)/shard_map/ppermute | solution.py:24
  278.0 12.4 %collective-permute-start.2 = (bf16[6,1,64,512]{3,2,1,0:T(8,128)(2,1)S(1)}, bf16[6,1,64,512]{3,2,1,0:T(8,128)(2,1)S(1)}, u32[]{:S(2)}, u32[]{:S(2)}) collective-permute-start(bf16[6,1,64,512]{3,2,1,0:T(8,128)(2,1)S(1)} %get-tuple-element.184), channel_id=1, source_target_pairs={{0,4},{4,8},{8,12},{12,16},{16,20},{20,24},{24,28},{1,5},{5,9},{9,... | collective-permute-start | bytes 1179656 | tf_op jit(solution)/shard_map/ppermute | solution.py:22
  282.0 16.7 %collective-permute-start.3 = (bf16[6,1,64,512]{3,2,1,0:T(8,128)(2,1)S(1)}, bf16[6,1,64,512]{3,2,1,0:T(8,128)(2,1)S(1)}, u32[]{:S(2)}, u32[]{:S(2)}) collective-permute-start(bf16[6,1,64,512]{3,2,1,0:T(8,128)(2,1)S(1)} %get-tuple-element.185), channel_id=1, source_target_pairs={{4,0},{8,4},{12,8},{16,12},{20,16},{24,20},{28,24},{5,1},{9,5},{13... | collective-permute-start | bytes 1179656 | tf_op jit(solution)/shard_map/ppermute | solution.py:24
  351.1 253.8 %copy-start.13 = (f32[512]{0:T(512)}, f32[512]{0:T(512)S(1)}, u32[]{:S(2)}) copy-start(f32[512]{0:T(512)S(1)} %broadcast_divide_fusion.3) | copy-start | bytes 6148
  394.9 210.0 %copy-start.19 = (f32[512]{0:T(512)}, f32[512]{0:T(512)S(1)}, u32[]{:S(2)}) copy-start(f32[512]{0:T(512)S(1)} %get-tuple-element.166) | copy-start | bytes 6148
  394.9 49.7 %copy-start.49 = (s32[20]{0:T(128)S(1)}, s32[20]{0:T(128)}, u32[]{:S(2)}) copy-start(s32[20]{0:T(128)} %param.23) | copy-start | bytes 244
  397.6 207.4 %copy-start.28 = (f32[512,1]{0,1:T(1,128)S(1)}, f32[512,1]{0,1:T(1,128)}, u32[]{:S(2)}) copy-start(f32[512,1]{0,1:T(1,128)} %copy-done.27) | copy-start | bytes 6148
  431.0 178.3 %copy-start.9 = (f32[12,512]{1,0:T(8,128)}, f32[12,512]{1,0:T(8,128)S(1)}, u32[]{:S(2)}) copy-start(f32[12,512]{1,0:T(8,128)S(1)} %broadcast_divide_fusion) | copy-start | bytes 73732
  662.2 22.8 %collective-permute-start.8 = (bf16[6,1,64,512]{3,2,1,0:T(8,128)(2,1)}, bf16[6,1,64,512]{3,2,1,0:T(8,128)(2,1)}, u32[]{:S(2)}, u32[]{:S(2)}) collective-permute-start(bf16[6,1,64,512]{3,2,1,0:T(8,128)(2,1)} %get-tuple-element.178), channel_id=1, source_target_pairs={{0,4},{4,8},{8,12},{12,16},{16,20},{20,24},{24,28},{1,5},{5,9},{9,... | collective-permute-start | bytes 1179656 | tf_op jit(solution)/shard_map/ppermute | solution.py:22
  666.7 25.8 %collective-permute-start.9 = (bf16[6,1,64,512]{3,2,1,0:T(8,128)(2,1)}, bf16[6,1,64,512]{3,2,1,0:T(8,128)(2,1)S(1)}, u32[]{:S(2)}, u32[]{:S(2)}) collective-permute-start(bf16[6,1,64,512]{3,2,1,0:T(8,128)(2,1)} %get-tuple-element.179), channel_id=1, source_target_pairs={{4,0},{8,4},{12,8},{16,12},{20,16},{24,20},{28,24},{5,1},{9,5},{13... | collective-permute-start | bytes 1179656 | tf_op jit(solution)/shard_map/ppermute | solution.py:24
  671.4 24.4 %collective-permute-start.12 = (bf16[6,1,64,512]{3,2,1,0:T(8,128)(2,1)S(1)}, bf16[6,1,64,512]{3,2,1,0:T(8,128)(2,1)S(1)}, u32[]{:S(2)}, u32[]{:S(2)}) collective-permute-start(bf16[6,1,64,512]{3,2,1,0:T(8,128)(2,1)S(1)} %get-tuple-element.180), channel_id=1, source_target_pairs={{0,4},{4,8},{8,12},{12,16},{16,20},{20,24},{24,28},{1,5},{5,9},{9,... | collective-permute-start | bytes 1179656 | tf_op jit(solution)/shard_map/ppermute | solution.py:22
  673.8 27.0 %collective-permute-start.13 = (bf16[6,1,64,512]{3,2,1,0:T(8,128)(2,1)S(1)}, bf16[6,1,64,512]{3,2,1,0:T(8,128)(2,1)S(1)}, u32[]{:S(2)}, u32[]{:S(2)}) collective-permute-start(bf16[6,1,64,512]{3,2,1,0:T(8,128)(2,1)S(1)} %get-tuple-element.181), channel_id=1, source_target_pairs={{4,0},{8,4},{12,8},{16,12},{20,16},{24,20},{28,24},{5,1},{9,5},{13... | collective-permute-start | bytes 1179656 | tf_op jit(solution)/shard_map/ppermute | solution.py:24
  684.7 287.3 %reduce-scatter.3.cloned.1.call-start = ((), (), s32[]{:S(2)}) async-start(), calls=%async_computation.4 | async-start | bytes 9732096 | tf_op jit(solution)/shard_map/reduce_scatter | solution.py:270
  710.8 52.6 %copy-start.29 = (f32[512]{0:T(512)S(1)}, f32[512]{0:T(512)}, u32[]{:S(2)}) copy-start(f32[512]{0:T(512)} %get-tuple-element.207) | copy-start | bytes 6148
  791.0 17.8 %collective-permute-start.10 = (bf16[6,1,64,512]{3,2,1,0:T(8,128)(2,1)S(1)}, bf16[6,1,64,512]{3,2,1,0:T(8,128)(2,1)S(1)}, u32[]{:S(2)}, u32[]{:S(2)}) collective-permute-start(bf16[6,1,64,512]{3,2,1,0:T(8,128)(2,1)S(1)} %get-tuple-element.174), channel_id=1, source_target_pairs={{0,4},{4,8},{8,12},{12,16},{16,20},{20,24},{24,28},{1,5},{5,9},{9,... | collective-permute-start | bytes 1179656 | tf_op jit(solution)/shard_map/ppermute | solution.py:22
  794.9 31.7 %collective-permute-start.11 = (bf16[6,1,64,512]{3,2,1,0:T(8,128)(2,1)S(1)}, bf16[6,1,64,512]{3,2,1,0:T(8,128)(2,1)S(1)}, u32[]{:S(2)}, u32[]{:S(2)}) collective-permute-start(bf16[6,1,64,512]{3,2,1,0:T(8,128)(2,1)S(1)} %get-tuple-element.175), channel_id=1, source_target_pairs={{4,0},{8,4},{12,8},{16,12},{20,16},{24,20},{28,24},{5,1},{9,5},{13... | collective-permute-start | bytes 1179656 | tf_op jit(solution)/shard_map/ppermute | solution.py:24
  797.8 30.2 %collective-permute-start.14 = (bf16[6,1,64,512]{3,2,1,0:T(8,128)(2,1)S(1)}, bf16[6,1,64,512]{3,2,1,0:T(8,128)(2,1)S(1)}, u32[]{:S(2)}, u32[]{:S(2)}) collective-permute-start(bf16[6,1,64,512]{3,2,1,0:T(8,128)(2,1)S(1)} %get-tuple-element.176), channel_id=1, source_target_pairs={{0,4},{4,8},{8,12},{12,16},{16,20},{20,24},{24,28},{1,5},{5,9},{9,... | collective-permute-start | bytes 1179656 | tf_op jit(solution)/shard_map/ppermute | solution.py:22
  800.8 31.9 %collective-permute-start.15 = (bf16[6,1,64,512]{3,2,1,0:T(8,128)(2,1)S(1)}, bf16[6,1,64,512]{3,2,1,0:T(8,128)(2,1)S(1)}, u32[]{:S(2)}, u32[]{:S(2)}) collective-permute-start(bf16[6,1,64,512]{3,2,1,0:T(8,128)(2,1)S(1)} %get-tuple-element.177), channel_id=1, source_target_pairs={{4,0},{8,4},{12,8},{16,12},{20,16},{24,20},{28,24},{5,1},{9,5},{13... | collective-permute-start | bytes 1179656 | tf_op jit(solution)/shard_map/ppermute | solution.py:24
  (49 other events, 564.8 us)
Sparse Core Ops, SparseCore 0:
  10.9 77.8 all-gather.4
  91.7 62.6 all-gather.6
  684.9 144.4 reduce-scatter.4
  836.7 135.3 reduce-scatter.2
where the time goes:
time: 992 us; the launch traced here: 979 us
  blocking collectives  400 us (40%)
  waiting for transfers between devices  173 us (17%)
  matrix products  127 us (13%)
  loops' own time  80.9 us (8%)
  other arithmetic  65.8 us (7%)
  local copies, waits for them, and re-layouts  61.6 us (6%)
  starting transfers between devices  55.8 us (6%)
  between operations  15.9 us (2%)
    reduce_scatter x1, waiting for transfers between devices, on_device(): lax.psum_scatter(term_one, ('gx', 'gy'), scatter_dimension=0, tiled=True)  125 us
    psum x2, blocking collectives, batch_statistics(): lax.psum(jnp.sum(values * inner_result, axis=(0, 1, 2)), ('gx', 'gy'))  82.7 us
    psum x2, blocking collectives, batch_statistics(): lax.psum(jnp.sum(inner_result * centered * centered, axis=(0, 1, 2)), ('g...  82.4 us
    psum x2, blocking collectives, norm_backward(): lax.psum((jnp.sum(output_gradient, axis=(0, 1, 2)), jnp.sum(output_gradie...  82.4 us
    another operation x1, loops' own time, frank_wolfe(): return lax.fori_loop(0, STEPS, fw_step, start)  80.9 us
    dot_general x8, matrix products, conv_rows(): output = jnp.dot(patches, weight, preferred_element_type=jnp.float32)  43.3 us
    ppermute x8, waiting for transfers between devices, extended(): lax.ppermute(head, axis, [((i + 1) % count, i) for i in range(ends)])  43.3 us
    all_gather x1, blocking collectives, weights_now(): lax.all_gather(head_weight, ('gx', 'gy'), axis=0, tiled=True)  37.7 us
  transfers between devices with their start and end apart: 20, of which 8 were waited for; matrix products, arithmetic and copies ran while one was open for 13% of the time, Pallas kernels for 0%

commit v1 on v0

--- a/solution.py
+++ b/solution.py
@@ -1,14 +1,924 @@
+import functools
+
 import jax
 import jax.numpy as jnp
 from jax import lax
+from jax.experimental import pallas as pl
+from jax.experimental.pallas import tpu as pltpu
 from jax.sharding import PartitionSpec as P
 
 TASKS = 40
 MICRO = 2
 STEPS = 20
-
-
 norm_eps = 1e-05
+BF = jnp.bfloat16
+F32 = jnp.float32
+HIGH = lax.Precision.HIGHEST
+MESH = pl.DeviceIdType.MESH
+
+C = 512
+COLS = 64
+PER = 6
+ROWS = 4
+SHARD = 144
+CUT = 80
+
+
+class Here:
+    def __init__(self):
+        gx = lax.axis_index("gx")
+        gy = lax.axis_index("gy")
+        self.z = lax.div(gx, 2)
+        self.y = lax.rem(gx, 2)
+        self.x = lax.div(gy, 2)
+        self.c = lax.rem(gy, 2)
+        self.gy = gy
+
+    def _fill(self, z, y, x, c):
+        return (
+            self.z if z is None else z,
+            self.y if y is None else y,
+            self.x if x is None else x,
+            self.c if c is None else c,
+        )
+
+    def dev(self, z=None, y=None, x=None, c=None):
+        z, y, x, c = self._fill(z, y, x, c)
+        return {"gx": z * 2 + y, "gy": x * 2 + c}
+
+    def idx(self, z=None, y=None, x=None, c=None):
+        z, y, x, c = self._fill(z, y, x, c)
+        return ((z * 2 + y) * 2 + x) * 2 + c
+
+    def near(self, j):
+        z = self.z
+        if j == 0:
+            return z
+        if j == 1:
+            return z + 1 - 2 * lax.rem(z, 2)
+        if j == 2:
+            return 2 - lax.div(z, 2)
+        return 3 - 3 * lax.div(z, 2)
+
+    def other(self, dy, dx, dc):
+        return (
+            1 - self.y if dy else self.y,
+            1 - self.x if dx else self.x,
+            1 - self.c if dc else self.c,
+        )
+
+    def ydev(self):
+        return self.dev(y=1 - self.y)
+
+    def xdev(self):
+        return self.dev(x=1 - self.x)
+
+    def sib(self):
+        return self.dev(c=1 - self.c)
+
+
+def rcopy(src, dst, ss, rs, dev):
+    return pltpu.make_async_remote_copy(
+        src_ref=src, dst_ref=dst, send_sem=ss, recv_sem=rs, device_id=dev, device_id_type=MESH
+    )
+
+
+class Gather:
+    def __init__(self, h, own, out, ss, rs, lsem, rows, cut, sent):
+        self.h, self.own, self.out, self.ss, self.rs = h, own, out, ss, rs
+        self.lsem, self.rows, self.cut, self.sent = lsem, rows, cut, sent
+        self.split = cut < rows
+
+    def at(self, i, lo=0, n=None):
+        n = self.rows if n is None else n
+        return self.out.at[pl.ds(pl.multiple_of(i * self.rows + lo, 16), n)]
+
+    def send(self, k, i, dev, lo=0, n=None, src=None, rk=None):
+        d = self.at(i, lo, n)
+        cp = rcopy(d if src is None else src, d, self.ss.at[k], self.rs.at[k if rk is None else rk], dev)
+        cp.start()
+        self.sent.append(cp)
+
+    def recv(self, k, i, lo=0, n=None):
+        d = self.at(i, lo, n)
+        rcopy(d, d, self.ss.at[0], self.rs.at[k], self.h.sib()).wait_recv()
+
+    def start(self):
+        h = self.h
+        me = h.idx()
+        self.local = pltpu.make_async_copy(self.own, self.at(me), self.lsem)
+        self.local.start()
+        for j in (1, 2, 3):
+            self.send(j - 1, me, h.dev(z=h.near(j)), src=self.own, rk=39 + h.z)
+        self.fan(0)
+
+    def fan(self, j):
+        h = self.h
+        i = h.idx(z=h.near(j))
+        src = self.own if j == 0 else None
+        if j:
+            self.recv(39 + h.near(j), i)
+        self.send(3 + j, i, h.ydev(), src=src)
+        self.send(7 + j, i, h.xdev(), src=src)
+        self.send(11 + j, i, h.sib(), src=src)
+
+    def second(self, j):
+        h = self.h
+        zz = h.near(j)
+        i = h.idx(z=zz, y=1 - h.y)
+        self.recv(3 + j, i)
+        self.send(15 + j, i, h.xdev(), 0, self.cut)
+        self.send(19 + j, i, h.sib())
+        i = h.idx(z=zz, x=1 - h.x)
+        self.recv(7 + j, i)
+        if self.split:
+            self.send(23 + j, i, h.ydev(), self.cut, self.rows - self.cut)
+        self.send(27 + j, i, h.sib())
+
+    def third(self, j):
+        h = self.h
+        i = h.idx(z=h.near(j), y=1 - h.y, x=1 - h.x)
+        self.recv(15 + j, i, 0, self.cut)
+        self.send(31 + j, i, h.sib(), 0, self.cut)
+        if self.split:
+            self.recv(23 + j, i, self.cut, self.rows - self.cut)
+            self.send(35 + j, i, h.sib(), self.cut, self.rows - self.cut)
+
+    def steps(self):
+        f, s, t = self.fan, self.second, self.third
+        order = [(f, 1), (s, 0), (f, 2), (s, 1), (t, 0), (f, 3), (s, 2), (t, 1), (s, 3), (t, 2), (t, 3)]
+        return [functools.partial(fn, j) for fn, j in order]
+
+    def finish(self):
+        h = self.h
+        c = 1 - h.c
+        for j in range(4):
+            zz = h.near(j)
+            self.recv(11 + j, h.idx(z=zz, c=c))
+            self.recv(19 + j, h.idx(z=zz, y=1 - h.y, c=c))
+            self.recv(27 + j, h.idx(z=zz, x=1 - h.x, c=c))
+            i = h.idx(z=zz, y=1 - h.y, x=1 - h.x, c=c)
+            self.recv(31 + j, i, 0, self.cut)
+            if self.split:
+                self.recv(35 + j, i, self.cut, self.rows - self.cut)
+        self.local.wait()
+
+
+class Scatter:
+    def __init__(self, h, dw, l1, lxa, lyb, lya, lxb, lz, ss, rs, out, sent):
+        self.h, self.dw, self.l1, self.lxa, self.lyb = h, dw, l1, lxa, lyb
+        self.lya, self.lxb, self.lz, self.ss, self.rs = lya, lxb, lz, ss, rs
+        self.out, self.sent = out, sent
+
+    def at(self, i, lo=0, n=SHARD):
+        return self.dw.at[pl.ds(pl.multiple_of(i * SHARD + lo, 16), n)]
+
+    def send(self, k, src, dst, dev):
+        cp = rcopy(src, dst, self.ss.at[k], self.rs.at[k], dev)
+        cp.start()
+        self.sent.append(cp)
+
+    def take(self, k, land, i, lo=0, n=SHARD):
+        rcopy(land, land, self.ss.at[0], self.rs.at[k], self.h.sib()).wait_recv()
+        d = self.at(i, lo, n)
+        d[...] = (d[...].astype(F32) + land[...].astype(F32)).astype(BF)
+
+    def s1(self, q):
+        h = self.h
+        for j in range(4):
+            self.send(4 * q + j, self.at(h.idx(q, j // 2, j % 2, 1 - h.c)), self.l1.at[q, j], h.sib())
+
+    def s2(self, q):
+        h = self.h
+        for j in range(4):
+            self.take(4 * q + j, self.l1.at[q, j], h.idx(q, j // 2, j % 2))
+        for j in range(2):
+            self.send(16 + 2 * q + j, self.at(h.idx(q, j, 1 - h.x), 0, CUT), self.lxa.at[q, j], h.xdev())
+            self.send(24 + 2 * q + j, self.at(h.idx(q, 1 - h.y, j), CUT, SHARD - CUT), self.lyb.at[q, j], h.ydev())
+
+    def s3(self, q):
+        h = self.h
+        for j in range(2):
+            self.take(16 + 2 * q + j, self.lxa.at[q, j], h.idx(q, j), 0, CUT)
+            self.take(24 + 2 * q + j, self.lyb.at[q, j], h.idx(q, h.y, j), CUT, SHARD - CUT)
+        self.send(32 + q, self.at(h.idx(q, 1 - h.y), 0, CUT), self.lya.at[q], h.ydev())
+        self.send(36 + q, self.at(h.idx(q, h.y, 1 - h.x), CUT, SHARD - CUT), self.lxb.at[q], h.xdev())
+
+    def _zcopy(self, q):
+        h = self.h
+        return rcopy(self.at(h.idx(q)), self.lz.at[h.z], self.ss.at[40 + q], self.rs.at[44 + h.z], h.dev(z=q))
+
+    def s4(self, q):
+        h = self.h
+        i = h.idx(q)
+        self.take(32 + q, self.lya.at[q], i, 0, CUT)
+        self.take(36 + q, self.lxb.at[q], i, CUT, SHARD - CUT)
+
+        @pl.when(h.z != q)
+        def _():
+            self._zcopy(q).start()
+
+    def finish(self, extra):
+        h = self.h
+        total = self.at(h.idx())[...].astype(F32) + extra
+        for j in (1, 2, 3):
+            zz = h.near(j)
+            land = self.lz.at[zz]
+            rcopy(land, land, self.ss.at[0], self.rs.at[44 + zz], h.sib()).wait_recv()
+            total = total + land[...].astype(F32)
+        self.out[...] = total
+
+    def drain(self):
+        h = self.h
+        for q in range(4):
+
+            @pl.when(h.z != q)
+            def _(q=q):
+                self._zcopy(q).wait_send()
+
+    def steps(self):
+        p = functools.partial
+        return [
+            [p(self.s1, 0)],
+            [p(self.s2, 0), p(self.s1, 1)],
+            [p(self.s3, 0), p(self.s2, 1), p(self.s1, 2)],
+            [p(self.s4, 0), p(self.s3, 1), p(self.s2, 2), p(self.s1, 3)],
+            [p(self.s4, 1), p(self.s3, 2), p(self.s2, 3)],
+            [p(self.s4, 2), p(self.s3, 3)],
+            [p(self.s4, 3)],
+        ]
+
+
+class Halo:
+    def __init__(self, h, edges, land, ss, rs):
+        self.h, self.land, self.ss, self.rs = h, land, ss, rs
+        self.up = rcopy(edges.at[0], land.at[1], ss.at[0], rs.at[0], h.dev(z=h.z - 1))
+        self.down = rcopy(edges.at[1], land.at[0], ss.at[1], rs.at[1], h.dev(z=h.z + 1))
+
+    def start(self):
+        pl.when(self.h.z > 0)(self.up.start)
+        pl.when(self.h.z < 3)(self.down.start)
+
+    def wait(self):
+        @pl.when(self.h.z > 0)
+        def _():
+            self.up.wait_send()
+            self.down.wait_recv()
+
+        @pl.when(self.h.z < 3)
+        def _():
+            self.down.wait_send()
+            self.up.wait_recv()
+
+
+class Sums:
+    def __init__(self, h, buf, ss, rs, sent):
+        self.h, self.buf, self.ss, self.rs, self.sent = h, buf, ss, rs, sent
+
+    def start_plane(self, payload):
+        h = self.h
+        self.own = payload
+        mine = self.buf.at[2, 0]
+        mine[...] = payload
+        for r in (1, 2, 3):
+            _, x, c = h.other(0, r // 2, r % 2)
+            cp = rcopy(mine, self.buf.at[0, h.gy], self.ss.at[r - 1], self.rs.at[r - 1], h.dev(x=x, c=c))
+            cp.start()
+            self.sent.append(cp)
+
+    def plane(self):
+        h = self.h
+        for r in (1, 2, 3):
+            _, x, c = h.other(0, r // 2, r % 2)
+            land = self.buf.at[0, x * 2 + c]
+            rcopy(land, land, self.ss.at[0], self.rs.at[r - 1], h.sib()).wait_recv()
+        return [jnp.where(h.gy == g, self.own, self.buf[0, g]) for g in range(4)]
+
+    def start_z(self, payload):
+        h = self.h
+        self.own = payload
+        mine = self.buf.at[2, 1]
+        mine[...] = payload
+        for j in (1, 2, 3):
+            cp = rcopy(mine, self.buf.at[1, h.z], self.ss.at[2 + j], self.rs.at[3 + h.z], h.dev(z=h.near(j)))
+            cp.start()
+            self.sent.append(cp)
+
+    def along_z(self):
+        h = self.h
+        for j in (1, 2, 3):
+            land = self.buf.at[1, h.near(j)]
+            rcopy(land, land, self.ss.at[0], self.rs.at[3 + h.near(j)], h.sib()).wait_recv()
+        return [jnp.where(h.z == g, self.own, self.buf[1, g]) for g in range(4)]
+
+
+def fold(row):
+    return [row[:, 128 * k : 128 * (k + 1)] for k in range(4)]
+
+
+def pack_rows(*rows):
+    rows = rows + (jnp.zeros((1, C), F32),) * (4 - len(rows))
+    return jnp.concatenate([part for r in rows for part in fold(r)], axis=0)
+
+
+def unpack_rows(p):
+    return [jnp.concatenate([p[4 * n + k : 4 * n + k + 1] for k in range(4)], axis=1) for n in range(p.shape[0] // 4)]
+
+
+def column(r):
+    return jnp.broadcast_to(r, (128, C)).T
+
+
+def merge(parts, counts):
+    total = sum(counts)
+    mass = sum(parts[g][0:4] for g in range(4))
+    mean = mass / jnp.maximum(total, 1.0)
+    spread = jnp.zeros_like(mass)
+    for g in range(4):
+        n = jnp.maximum(counts[g], 1.0)
+        gap = parts[g][0:4] / n - mean
+        spread = spread + parts[g][4:8] + counts[g] * gap * gap
+    third = parts[0] + parts[1] + parts[2] + parts[3]
+    return jnp.concatenate([mass, spread, third[8:16]], axis=0)
+
+
+def nn(a, b):
+    return lax.dot_general(a, b, (((1,), (0,)), ((), ())), preferred_element_type=F32)
+
+
+def nt(a, b):
+    return lax.dot_general(a, b, (((1,), (1,)), ((), ())), preferred_element_type=F32)
+
+
+def tn(a, b):
+    return lax.dot_general(a, b, (((0,), (0,)), ((), ())), preferred_element_type=F32)
+
+
+def sigmoid(u):
+    return 1.0 / (1.0 + jnp.exp(-u))
+
+
+def body(
+    feat, w1s, w2s, gain, bias, head, hbias, labels, spans, heights, widths, picks,
+    pooled_out, fg_out, c1_out, c2_out, gg_out, bg_out, hg_out, hbg_out,
+    w1, w2, x3, first, second, slope, dh, base, hid, dw,
+    al, edges, bland, hland, sland, fland, fgs, fgl,
+    e32, exts, ext, gb, stat, pacc, pz, pg, res, cot, yb, ht, gsc, mc1, mc2,
+    l1, lxa, lyb, lya, lxb, lz,
+    sem_g, rem_g, sem_ge, rem_ge, sem_l, sem_h, rem_h, sem_s, rem_s, sem_a, rem_a, sem_p, rem_p, sem_r, rem_r,
+):
+    h = Here()
+    sent = []
+    z, y = h.z, h.y
+
+    barrier = pltpu.get_barrier_semaphore()
+    peers = [h.dev(z=h.near(j)) for j in (1, 2, 3)]
+    for r in range(1, 8):
+        yy, xx, cc = h.other(r // 4, (r // 2) % 2, r % 2)
+        peers.append(h.dev(y=yy, x=xx, c=cc))
+    for dev in peers:
+        pl.semaphore_signal(barrier, inc=1, device_id=dev, device_id_type=MESH)
+    pl.semaphore_wait(barrier, len(peers))
+
+    a2a = rcopy(feat.at[pl.ds(PER * (1 - y), PER)], al, sem_a.at[0], rem_a.at[0], h.ydev())
+    a2a.start()
+    g1 = Gather(h, w1s, w1, sem_g.at[0], rem_g.at[0], sem_l.at[0], SHARD, CUT, sent)
+    sent2 = []
+    g2 = Gather(h, w2s, w2, sem_g.at[1], rem_g.at[1], sem_l.at[1], SHARD, CUT, sent2)
+    ge = Gather(h, exts, ext, sem_ge, rem_ge, sem_l.at[2], 16, 16, sent)
+    g1.start()
+    e32[...] = jnp.zeros_like(e32)
+    e32[:, 0:2] = gain[...].astype(F32)
+    e32[:, 128:130] = bias[...].astype(F32)
+    e32[:, 256 : 256 + TASKS] = head[...].astype(F32)
+    e32[0:12, 384 : 384 + TASKS] = labels[...].astype(F32)
+    exts[...] = e32[...].astype(BF)
+    ge.start()
+
+    image = lax.broadcasted_iota(jnp.int32, (1, 8 * PER), 1)
+    high, broad = spans[0:1], spans[1:2]
+
+    def pixels(zz, lo, n):
+        here = (image >= lo) & (image < lo + n)
+        cells = jnp.where(here, jnp.clip(high - ROWS * zz, 0, ROWS) * broad, 0).astype(F32)
+        return cells.sum(1, keepdims=True)
+
+    n_plane = [pixels(z, 2 * PER * g + PER * y, PER) for g in range(4)]
+    n_z = [sum(pixels(zz, 2 * PER * g + PER * y, PER) for g in range(4)) for zz in range(4)]
+    total = sum(n_z)
+    my_first = h.gy * 2 * PER + PER * y
+
+    col = lax.broadcasted_iota(jnp.int32, (COLS, C), 0)
+
+    def wide(i, r):
+        return jnp.where(ROWS * z + r < heights[my_first + i], widths[my_first + i], 0)
+
+    def keep(i, r, v):
+        return jnp.where(col < wide(i, r), v, 0.0)
+
+    zero8 = jnp.zeros((8, C), F32)
+
+    def by8(v):
+        return v.reshape(COLS // 8, 8, C).sum(0)
+
+    def put3(i, row, v):
+        x3[i, row, :, C : 2 * C] = v.astype(BF)
+        x3[i, row, :, 0:C] = jnp.where(col == 0, 0.0, pltpu.roll(v, 1, 0)).astype(BF)
+        x3[i, row, :, 2 * C : 3 * C] = jnp.where(col == COLS - 1, 0.0, pltpu.roll(v, COLS - 1, 0)).astype(BF)
+
+    def put_halo(land):
+        def one(i, _):
+            @pl.when(z > 0)
+            def _():
+                put3(i, 0, land[0, i].astype(F32))
+
+            @pl.when(z == 0)
+            def _():
+                x3[i, 0] = jnp.zeros((COLS, 3 * C), BF)
+
+            @pl.when(z < 3)
+            def _():
+                put3(i, 5, land[1, i].astype(F32))
+
+            @pl.when(z == 3)
+            def _():
+                x3[i, 5] = jnp.zeros((COLS, 3 * C), BF)
+
+            return 0
+
+        lax.fori_loop(0, PER, one, 0)
+
+    def take_rows(src, offset, row0):
+        def one(i, acc):
+            for r in range(2):
+                v = keep(i, row0 + r, src[offset + i, r].astype(F32))
+                base[i, row0 + r] = v.astype(BF)
+                put3(i, row0 + r + 1, v)
+                acc = acc + by8(v)
+            return acc
+
+        return lax.fori_loop(0, PER, one, zero8)
+
+    steps = g1.steps()
+
+    def go(todo, n):
+        for _ in range(min(n, len(todo))):
+            todo.pop(0)()
+
+    base_sum = take_rows(feat, PER * y, 2 * y)
+    go(steps, 5)
+    a2a.wait_recv()
+    base_sum = (base_sum + take_rows(al, 0, 2 * (1 - y))).sum(0, keepdims=True)
+    edges[0] = base[:, 0]
+    edges[1] = base[:, ROWS - 1]
+    halo = Halo(h, edges, bland, sem_h.at[0], rem_h.at[0])
+    halo.start()
+    go(steps, 99)
+    for step in ge.steps():
+        step()
+    ge.finish()
+    g1.finish()
+    g2.start()
+    steps = g2.steps()
+
+    gb[0:2] = ext[:, 0:128].astype(F32).T[0:2]
+    gb[2:4] = ext[:, 128:256].astype(F32).T[0:2]
+    ht[...] = ext[:, 256:384].astype(F32)
+
+    def conv(w, out, land, halo, todo=()):
+        todo = list(todo)
+        for p in range(3):
+            im = pl.ds(2 * p, 2)
+            mid = nn(x3[im, 1:5].reshape(8 * COLS, 3 * C), w[3 * C : 6 * C]).reshape(2, 4, COLS, C)
+            lo = nn(x3[im, 1:4].reshape(6 * COLS, 3 * C), w[0 : 3 * C]).reshape(2, 3, COLS, C)
+            hi = nn(x3[im, 2:5].reshape(6 * COLS, 3 * C), w[6 * C : 9 * C]).reshape(2, 3, COLS, C)
+            out[im, 0] = mid[:, 0] + hi[:, 0]
+            out[im, 1] = mid[:, 1] + lo[:, 0] + hi[:, 1]
+            out[im, 2] = mid[:, 2] + lo[:, 1] + hi[:, 2]
+            out[im, 3] = mid[:, 3] + lo[:, 2]
+            if todo:
+                todo.pop(0)()
+        halo.wait()
+        put_halo(land)
+        out[:, 0] += nn(x3[:, 0].reshape(6 * COLS, 3 * C), w[0 : 3 * C]).reshape(PER, COLS, C)
+        out[:, 3] += nn(x3[:, 5].reshape(6 * COLS, 3 * C), w[6 * C : 9 * C]).reshape(PER, COLS, C)
+
+    def conv_back(w, out, land, halo, todo=()):
+        todo = list(todo)
+
+        def taps(lhs, a):
+            acc = None
+            for b in range(3):
+                part = nt(lhs[:, (2 - b) * C : (3 - b) * C], w[(3 * a + b) * C : (3 * a + b + 1) * C])
+                acc = part if acc is None else acc + part
+            return acc
+
+        for p in range(3):
+            im = pl.ds(2 * p, 2)
+            mid = taps(x3[im, 1:5].reshape(8 * COLS, 3 * C), 1).reshape(2, 4, COLS, C)
+            lo = taps(x3[im, 1:4].reshape(6 * COLS, 3 * C), 2).reshape(2, 3, COLS, C)
+            hi = taps(x3[im, 2:5].reshape(6 * COLS, 3 * C), 0).reshape(2, 3, COLS, C)
+            out[im, 0] = mid[:, 0] + hi[:, 0]
+            out[im, 1] = mid[:, 1] + lo[:, 0] + hi[:, 1]
+            out[im, 2] = mid[:, 2] + lo[:, 1] + hi[:, 2]
+            out[im, 3] = mid[:, 3] + lo[:, 2]
+            if todo:
+                todo.pop(0)()
+        halo.wait()
+        put_halo(land)
+        out[:, 0] += taps(x3[:, 0].reshape(6 * COLS, 3 * C), 2).reshape(PER, COLS, C)
+        out[:, 3] += taps(x3[:, 5].reshape(6 * COLS, 3 * C), 0).reshape(PER, COLS, C)
+
+    def spread(src):
+        def one(i, carry):
+            n, mean, dev = carry
+            widths_i = [wide(i, r) for r in range(ROWS)]
+            ni = sum(widths_i).astype(F32)
+            mass = jnp.zeros((8, C), F32)
+            for r in range(ROWS):
+                v = jnp.where(col < widths_i[r], src[i, r], 0.0)
+                mass = mass + v.reshape(COLS // 8, 8, C).sum(0)
+            mi = mass.sum(0, keepdims=True) / jnp.maximum(ni, 1.0)
+            sq = jnp.zeros((8, C), F32)
+            for r in range(ROWS):
+                v = jnp.where(col < widths_i[r], src[i, r] - mi, 0.0)
+                sq = sq + (v * v).reshape(COLS // 8, 8, C).sum(0)
+            both = jnp.maximum(n + ni, 1.0)
+            gap = mi - mean
+            return (
+                n + ni,
+                mean + gap * (ni / both),
+                dev + sq.sum(0, keepdims=True) + gap * gap * (n * ni / both),
+            )
+
+        zero = jnp.zeros((1, C), F32)
+        n, mean, dev = lax.fori_loop(0, PER, one, (jnp.float32(0.0), zero, zero))
+        return mean * n, dev
+
+    def statistics(src, k, todo, inputs):
+        ex = Sums(h, stat.at[k], sem_s.at[k], rem_s.at[k], sent)
+        ex.start_plane(pack_rows(*spread(src), inputs))
+        go(todo, 1)
+        ex.start_z(merge(ex.plane(), n_plane))
+        go(todo, 1)
+        both = merge(ex.along_z(), n_z)
+        mass, dev, inputs, _ = unpack_rows(both)
+        return mass / total, lax.rsqrt(dev / total + norm_eps), inputs / total
+
+    def start_sums(k, *rows):
+        ex = Sums(h, stat.at[k], sem_s.at[k], rem_s.at[k], sent)
+        ex.start_plane(pack_rows(*rows))
+        return ex
+
+    def mid_sums(ex):
+        parts = ex.plane()
+        ex.start_z(parts[0] + parts[1] + parts[2] + parts[3])
+
+    def end_sums(ex):
+        parts = ex.along_z()
+        return parts[0] + parts[1] + parts[2] + parts[3]
+
+    def edges_first(one, start):
+        def edge(i, acc):
+            for k, r in enumerate((0, ROWS - 1)):
+                v = one(i, r)
+                edges[k, i] = v.astype(BF)
+                acc = acc + by8(v)
+            return acc
+
+        def inner(i, acc):
+            for r in range(1, ROWS - 1):
+                acc = acc + by8(one(i, r))
+            return acc
+
+        acc = lax.fori_loop(0, PER, edge, zero8)
+        start()
+        return lax.fori_loop(0, PER, inner, acc).sum(0, keepdims=True)
+
+    conv(w1, first, bland, halo, [steps.pop(0) for _ in range(3)])
+    center, rs1, base_mean = statistics(first, 0, steps, base_sum)
+    go(steps, 1)
+    gain1, bias1 = gb[0:1], gb[2:3]
+
+    def hidden(i, r):
+        xh = (first[i, r] - center) * rs1
+        first[i, r] = xh
+        u = gain1 * xh + bias1
+        v = keep(i, r, u * sigmoid(u))
+        hid[i, r] = v.astype(BF)
+        put3(i, r + 1, v)
+        return v
+
+    halo = Halo(h, edges, hland, sem_h.at[1], rem_h.at[1])
+    hid_sum = edges_first(hidden, halo.start)
+    go(steps, 99)
+    g2.finish()
+    conv(w2, second, hland, halo)
+    center, rs2, hid_mean = statistics(second, 1, [], hid_sum)
+    gain2, bias2 = gb[1:2], gb[3:4]
+
+    pacc[...] = jnp.zeros_like(pacc)
+
+    def finals(i, _):
+        acc = [jnp.zeros((8, C), F32) for _ in range(3)]
+        for r in range(ROWS):
+            xh = (second[i, r] - center) * rs2
+            second[i, r] = xh
+            pre = gain2 * xh + bias2 + base[i, r].astype(F32)
+            s = sigmoid(pre)
+            act = keep(i, r, pre * s)
+            sl = keep(i, r, s * (1.0 + pre * (1.0 - s)))
+            slope[i, r] = sl
+            for k, v in enumerate((act, sl, sl * xh)):
+                acc[k] = acc[k] + v.reshape(COLS // 8, 8, C).sum(0)
+        for k in range(3):
+            pacc[k, pl.ds(i, 1)] = acc[k].sum(0, keepdims=True)
+        return 0
+
+    lax.fori_loop(0, PER, finals, 0)
+
+    rows8 = lax.broadcasted_iota(jnp.int32, (8, 1), 0)
+    inv_pix = jnp.zeros((8, 1), F32)
+    for i in range(PER):
+        inv_pix = jnp.where(rows8 == i, 1.0 / (heights[my_first + i] * widths[my_first + i]).astype(F32), inv_pix)
+    me_z = pz.at[z]
+    me_z[...] = pacc[0]
+    for j in (1, 2, 3):
+        cp = rcopy(me_z, me_z, sem_p.at[j - 1], rem_p.at[z], h.dev(z=h.near(j)))
+        cp.start()
+        sent.append(cp)
+    head_gram = lax.dot_general(ht[...], ht[...], (((0,), (0,)), ((), ())), precision=HIGH, preferred_element_type=F32)
+    for j in (1, 2, 3):
+        land = pz.at[h.near(j)]
+        rcopy(land, land, sem_p.at[0], rem_p.at[h.near(j)], h.sib()).wait_recv()
+    slot = (y * 2 + h.x) * 2 + h.c
+    me_p = pg.at[slot]
+    me_p[...] = (pz[0] + pz[1] + pz[2] + pz[3]) * inv_pix
+    for r in range(1, 8):
+        yy, xx, cc = h.other(r // 4, (r // 2) % 2, r % 2)
+        cp = rcopy(me_p, me_p, sem_p.at[2 + r], rem_p.at[3 + r], h.dev(y=yy, x=xx, c=cc))
+        cp.start()
+        sent.append(cp)
+    lane = lax.broadcasted_iota(jnp.int32, (8, 128), 1)
+    row = lax.broadcasted_iota(jnp.int32, (8, 128), 0)
+    real = (row < PER) & (lane < TASKS)
+    wanted = []
+    for s in range(8):
+        yy, gy = s // 4, s % 4
+        lab = ext[16 * gy : 16 * gy + 16, 384:512].astype(F32)
+        lab = lab[PER * yy : PER * yy + PER]
+        wanted.append(jnp.concatenate([lab, jnp.zeros((2, 128), F32)], axis=0))
+    for r in range(1, 8):
+        yy, xx, cc = h.other(r // 4, (r // 2) % 2, r % 2)
+        land = pg.at[(yy * 2 + xx) * 2 + cc]
+        rcopy(land, land, sem_p.at[0], rem_p.at[3 + r], h.sib()).wait_recv()
+    pooled = pg[...].reshape(64, C)
+    offset = hbias[...].astype(F32)
+    logits = lax.dot_general(pooled, ht[...], (((1,), (0,)), ((), ())), precision=HIGH, preferred_element_type=F32)
+    logits = logits.reshape(8, 8, 128) + offset
+    images = 8 * PER
+    for s in range(8):
+        res[s] = jnp.where(real, (sigmoid(logits[s]) - wanted[s]) / images, 0.0)
+    residual = res[...].reshape(64, 128)
+    gram = head_gram * lax.dot_general(
+        residual, residual, (((0,), (0,)), ((), ())), precision=HIGH, preferred_element_type=F32
+    )
+    gram = gram[0:TASKS]
+    lane1 = lax.broadcasted_iota(jnp.int32, (1, 128), 1)
+    sub = lax.broadcasted_iota(jnp.int32, (TASKS, 128), 0)
+
+    def fw(k, carry):
+        mix, q = carry
+        t = picks[k]
+        one = (lane1 == t).astype(F32)
+        line = jnp.where(sub == t, gram, 0.0).sum(0, keepdims=True)
+        self_dot = (mix * q).sum(1, keepdims=True)
+        cross = (one * q).sum(1, keepdims=True)
+        vertex = (one * line).sum(1, keepdims=True)
+        d = jnp.maximum(self_dot + vertex - 2.0 * cross, 0.1 * vertex)
+        step = jnp.clip((self_dot - cross) / d, 0.0, 1.0)
+        return (1.0 - step) * mix + step * one, (1.0 - step) * q + step * line
+
+    mix0 = jnp.where(lane1 < TASKS, 1.0 / TASKS, 0.0)
+    mix, _ = lax.fori_loop(0, STEPS, fw, (mix0, gram.sum(0, keepdims=True) / TASKS))
+    mine = res[slot] * mix
+    cot[...] = inv_pix * lax.dot_general(
+        mine, ht[...], (((1,), (1,)), ((), ())), precision=HIGH, preferred_element_type=F32
+    )
+    ex = start_sums(
+        2, (cot[...] * pacc[1]).sum(0, keepdims=True), (cot[...] * pacc[2]).sum(0, keepdims=True)
+    )
+
+    for yy in range(2):
+        pooled_out[PER * yy : PER * (yy + 1)] = pg[(yy * 2 + h.x) * 2 + h.c][0:PER]
+    head_grad = lax.dot_general(
+        pooled, residual, (((0,), (0,)), ((), ())), precision=HIGH, preferred_element_type=F32
+    )
+    mid_sums(ex)
+    gsc[...] = head_grad
+    hg_out[...] = gsc[pl.ds(pl.multiple_of(h.idx() * 16, 16), 16)][:, 0:TASKS]
+    hbg_out[...] = residual.sum(0, keepdims=True)[:, 0:TASKS]
+    sums2 = end_sums(ex)
+    yb[0, 0:8] = sums2[0:8]
+    mc1[0:C] = column(base_mean)
+    mc1[C:] = mc1[0:256]
+    mc2[0:C] = column(hid_mean)
+    mc2[C:] = mc2[0:256]
+    yb[0, 24:32] = pack_rows(hid_mean, base_mean)[0:8]
+
+    sum_b, sum_g, _, _ = unpack_rows(sums2)
+    mean_b, mean_g = sum_b / total, sum_g / total
+    scale = gain2 * rs2
+
+    def d_second(i, r):
+        xh = second[i, r]
+        dp = slope[i, r] * cot[pl.ds(i, 1)]
+        v = keep(i, r, scale * (dp - mean_b - xh * mean_g))
+        put3(i, r + 1, v)
+        return v.astype(BF).astype(F32)
+
+    halo = Halo(h, edges, sland, sem_h.at[2], rem_h.at[2])
+    d2_sum = edges_first(d_second, halo.start)
+    conv_back(w2, dh, sland, halo)
+
+    def d_norm1(i, carry):
+        a, b = carry
+        for r in range(ROWS):
+            xh = first[i, r]
+            u = gain1 * xh + bias1
+            s = sigmoid(u)
+            v = keep(i, r, dh[i, r] * (s * (1.0 + u * (1.0 - s))))
+            dh[i, r] = v
+            a = a + v.reshape(COLS // 8, 8, C).sum(0)
+            b = b + (v * xh).reshape(COLS // 8, 8, C).sum(0)
+        return a, b
+
+    a, b = lax.fori_loop(0, PER, d_norm1, (zero8, zero8))
+    ex = start_sums(3, a.sum(0, keepdims=True), b.sum(0, keepdims=True), d2_sum)
+
+    def weight_taps(x, out, mean, d_sum, lo, hi):
+        for t in range(lo, hi):
+            ta, tb = t // 3, t % 3
+            d = x3[:, 2 - ta : 6 - ta, :, (2 - tb) * C : (3 - tb) * C].reshape(PER * ROWS * COLS, C)
+            part = tn(x[...].reshape(PER * ROWS * COLS, C), d)
+            off = jnp.concatenate([mean[0:C] * f for f in fold(d_sum)], axis=1)
+            out[t * C : (t + 1) * C] = (part - off).astype(BF)
+
+    def scatter(k, src, out):
+        return Scatter(
+            h, src, l1.at[k], lxa.at[k], lyb.at[k], lya.at[k], lxb.at[k], lz.at[k], sem_r.at[k], rem_r.at[k], out, sent
+        )
+
+    r2 = scatter(0, dw, c2_out)
+    todo2 = r2.steps()
+
+    def flush(todo, n=1):
+        for _ in range(min(n, len(todo))):
+            for step in todo.pop(0):
+                step()
+
+    weight_taps(hid, dw, mc2, d2_sum, 0, 3)
+    flush(todo2)
+    mid_sums(ex)
+    weight_taps(hid, dw, mc2, d2_sum, 3, 5)
+    flush(todo2)
+    weight_taps(hid, dw, mc2, d2_sum, 5, 7)
+    flush(todo2)
+    weight_taps(hid, dw, mc2, d2_sum, 7, 9)
+    flush(todo2)
+    sums1 = end_sums(ex)
+    yb[0, 8:20] = sums1[0:12]
+    sum_b, sum_g, _, _ = unpack_rows(sums1)
+    mean_b1, mean_g1 = sum_b / total, sum_g / total
+    scale1 = gain1 * rs1
+
+    def d_first(i, r):
+        v = keep(i, r, scale1 * (dh[i, r] - mean_b1 - first[i, r] * mean_g1))
+        put3(i, r + 1, v)
+        return v.astype(BF).astype(F32)
+
+    halo = Halo(h, edges, fland, sem_h.at[3], rem_h.at[3])
+    d1_sum = edges_first(d_first, halo.start)
+    ex = start_sums(4, d1_sum)
+    conv_back(w1, dh, fland, halo, [functools.partial(flush, todo2) for _ in range(3)])
+    mid_sums(ex)
+
+    def result(i, r):
+        return keep(i, r, dh[i, r] + slope[i, r] * cot[pl.ds(i, 1)])
+
+    back = []
+    for p in range(3):
+        for i in (2 * p, 2 * p + 1):
+            for r in range(2):
+                fgs[i, r] = result(i, 2 * (1 - y) + r).astype(BF)
+        im = pl.ds(2 * p, 2)
+        cp = rcopy(fgs.at[im], fgl.at[im], sem_a.at[2 + p], rem_a.at[2 + p], h.ydev())
+        cp.start()
+        back.append(cp)
+
+    def stay(i, _):
+        for r in range(2):
+            fg_out[PER * y + i, r] = result(i, 2 * y + r)
+        return 0
+
+    lax.fori_loop(0, PER, stay, 0)
+    flush(todo2, 99)
+    yb[0, 20:24] = end_sums(ex)[0:4]
+    ysum = rcopy(yb.at[0], yb.at[1], sem_a.at[1], rem_a.at[1], h.ydev())
+    ysum.start()
+
+    for cp in sent2:
+        cp.wait_send()
+    r1 = scatter(1, w2, c1_out)
+    todo1 = r1.steps()
+    weight_taps(base, w2, mc1, d1_sum, 0, 3)
+    flush(todo1)
+    weight_taps(base, w2, mc1, d1_sum, 3, 5)
+    flush(todo1)
+    weight_taps(base, w2, mc1, d1_sum, 5, 7)
+    flush(todo1)
+    weight_taps(base, w2, mc1, d1_sum, 7, 9)
+    flush(todo1)
+    flush(todo1)
+
+    ysum.wait_recv()
+    sb2, sg2, sb1, sg1 = unpack_rows(yb[0, 0:16] + yb[1, 0:16])
+    flat = jnp.concatenate([sg1, sg2, sb1, sb2, jnp.zeros((124, C), F32)], axis=0).T
+    gsc[...] = flat
+    own = gsc[pl.ds(pl.multiple_of(h.idx() * 16, 16), 16)]
+    gg_out[...] = own[:, 0:2]
+    bg_out[...] = own[:, 2:4]
+
+    at = pl.ds(pl.multiple_of(lax.rem(h.idx() * SHARD, C), 16), SHARD)
+    d2_all, d1_all, hid_other, base_other = unpack_rows(yb[1, 16:32])
+    d2_mine, d1_mine, _, _ = unpack_rows(yb[0, 16:32])
+
+    def taken_off(mean, other, all_mine, all_other):
+        off = jnp.concatenate([mean[at] * f for f in fold(all_mine)], axis=1)
+        mean[0:C] = column(other)
+        mean[C:] = mean[0:256]
+        return off + jnp.concatenate([mean[at] * f for f in fold(all_other)], axis=1)
+
+    off2 = taken_off(mc2, hid_other, d2_mine, d2_all)
+    off1 = taken_off(mc1, base_other, d1_mine, d1_all)
+    r2.finish(off2)
+    flush(todo1)
+    for p in range(3):
+        back[p].wait_recv()
+        for i in (2 * p, 2 * p + 1):
+            fg_out[PER * (1 - y) + i] = fgl[i].astype(F32)
+    flush(todo1, 99)
+    r1.finish(off1)
+
+    a2a.wait_send()
+    ysum.wait_send()
+    for cp in back + sent:
+        cp.wait_send()
+    r1.drain()
+    r2.drain()
+
+
+def fused(features, w1s, w2s, gain, bias, head, head_bias, labels, heights, widths, picks):
+    vm = pl.BlockSpec(memory_space=pltpu.VMEM)
+    sm = pl.BlockSpec(memory_space=pltpu.SMEM)
+    V = pltpu.VMEM
+    dma = pltpu.SemaphoreType.DMA
+    maps = (PER, ROWS, COLS, C)
+    edge = (2, PER, COLS, C)
+    half = (PER, 2, COLS, C)
+    scratch = [
+        V((9 * C, C), BF), V((9 * C, C), BF), V((PER, ROWS + 2, COLS, 3 * C), BF),
+        V(maps, F32), V(maps, F32), V(maps, F32), V(maps, F32), V(maps, BF), V(maps, BF), V((9 * C, C), BF),
+        V(half, BF), V(edge, BF), V(edge, BF), V(edge, BF), V(edge, BF), V(edge, BF), V(half, BF), V(half, BF),
+        V((16, C), F32), V((16, C), BF), V((C, C), BF), V((8, C), F32),
+        V((5, 3, 4, 16, 128), F32), V((3, 8, C), F32), V((4, 8, C), F32), V((8, 8, C), F32),
+        V((8, 8, 128), F32), V((8, C), F32), V((2, 32, 128), F32), V((C, 128), F32), V((C, 128), F32),
+        V((C + 256, 128), F32), V((C + 256, 128), F32),
+        V((2, 4, 4, SHARD, C), BF), V((2, 4, 2, CUT, C), BF), V((2, 4, 2, SHARD - CUT, C), BF),
+        V((2, 4, CUT, C), BF), V((2, 4, SHARD - CUT, C), BF), V((2, 4, SHARD, C), BF),
+        dma((2, 43)), dma((2, 43)), dma((43,)), dma((43,)), dma((3,)), dma((4, 2)), dma((4, 2)),
+        dma((5, 8)), dma((5, 8)), dma((5,)), dma((5,)), dma((12,)), dma((12,)), dma((2, 48)), dma((2, 48)),
+    ]
+    f = jax.ShapeDtypeStruct
+    outs = pl.pallas_call(
+        body,
+        out_shape=[
+            f((2 * PER, C), F32), f((2 * PER, 2, COLS, C), F32), f((SHARD, C), F32), f((SHARD, C), F32),
+            f((16, 2), F32), f((16, 2), F32), f((16, TASKS), F32), f((1, TASKS), F32),
+        ],
+        in_specs=[vm] * 9 + [sm] * 3,
+        out_specs=[vm] * 8,
+        scratch_shapes=scratch,
+        compiler_params=pltpu.CompilerParams(
+            collective_id=0, has_side_effects=True, vmem_limit_bytes=63 * 2**20
+        ),
+        name="block",
+    )(
+        features, w1s, w2s, gain, bias, head,
+        jnp.pad(head_bias.reshape(1, TASKS), ((0, 0), (0, 128 - TASKS))), labels,
+        jnp.stack([heights, widths]), heights, widths, picks,
+    )
+    return tuple(outs[:7]) + (outs[7].reshape(TASKS),)
 
 
 def extended(cells, sides, width):
@@ -314,6 +1224,7 @@
         P(("gx", "gy"), None),
         P(),
     )
+    whole = dict(mesh.shape) != {"gx": 8, "gy": 4}
     return jax.shard_map(
-        on_device, mesh=mesh, in_specs=in_specs, out_specs=out_specs, check_vma=False
-    )
+        on_device if whole else fused, mesh=mesh, in_specs=in_specs, out_specs=out_specs, check_vma=False
+    )

time: 992 us -> 257 us (0.26)
  blocking collectives: 400 us -> 0 us
  Pallas kernels: 0 us -> 237 us
  waiting for transfers between devices: 173 us -> 0 us
  matrix products: 127 us -> 0 us
  loops' own time: 80.9 us -> 0 us
  other arithmetic: 65.8 us -> 1.24 us
  starting transfers between devices: 55.8 us -> 0 us
  local copies, waits for them, and re-layouts: 61.6 us -> 14.5 us
  between operations: 15.9 us -> 0.84 us
    psum x8 -> x0, blocking collectives: 293 us -> none  [the longest x2 82.7 us: batch_statistics(): lax.psum(jnp.sum(values * inner_result, axis=(0, 1, 2)), ('gx', 'gy'))]
    pallas_call x0 -> x1, Pallas kernels: none -> 237 us  [fused(): pl.pallas_call(body, out_shape=[f((2 * PER, C), F32), f((2 * PER, 2, COLS...]
    dot_general x57 -> x0, matrix products: 127 us -> none  [the longest x8 43.3 us: conv_rows(): output = jnp.dot(patches, weight, preferred_element_type=jnp.float32)]
    reduce_scatter x2 -> x0, waiting for transfers between devices: 126 us -> none  [the longest x1 125 us: on_device(): lax.psum_scatter(term_one, ('gx', 'gy'), scatter_dimension=0, tiled=True)]
    all_gather x3 -> x0, blocking collectives: 107 us -> none  [the longest x1 37.7 us: weights_now(): lax.all_gather(head_weight, ('gx', 'gy'), axis=0, tiled=True)]
    another operation x1 -> x0, loops' own time: 80.9 us -> none  [frank_wolfe(): return lax.fori_loop(0, STEPS, fw_step, start)]
    ppermute x16 -> x0, starting transfers between devices: 55.4 us -> none  [the longest x8 27.9 us: extended(): lax.ppermute(tail, axis, [(i, (i + 1) % count) for i in range(ends)])]
    ppermute x16 -> x0, waiting for transfers between devices: 46.5 us -> none  [the longest x8 43.3 us: extended(): lax.ppermute(head, axis, [((i + 1) % count, i) for i in range(ends)])]
  transfers between devices with their start and end apart: 20 -> 0, of which waited for: 8 -> 0; matrix products, arithmetic and copies ran while one was open for 13% -> 0% of each run, Pallas kernels for 0% -> 0%
where the time goes in v1:
time: 257 us; the launch traced here: 253 us
  Pallas kernels  237 us (92%)
  local copies, waits for them, and re-layouts  14.5 us (6%)
    pallas_call x1, Pallas kernels, fused(): pl.pallas_call(body, out_shape=[f((2 * PER, C), F32), f((2 * PER, 2, COLS...  237 us
    unnamed x18, local copies, waits for them, and re-layouts  13.3 us

profile of v1, /device:TPU:24, one launch (start us, length us, event | category | flops | bytes accessed | tf_op | source)
XLA Modules:
  0.0 253.1 jit_solution(3973226838637595374)
XLA Ops:
  0.6 1.2 pad.4.hbias
  1.8 1.2 pad_add_fusion.spans
  3.0 1.3 copy.19.gain
  4.4 1.3 copy.20.bias
  5.7 236.5 %block.1 = (f32[12,512]{1,0:T(8,128)}, f32[12,2,64,512]{3,2,1,0:T(8,128)}, f32[144,512]{1,0:T(8,128)}, f32[144,512]{1,0:T(8,128)}, f32[16,2]{1,0:T(8,128)}, /*in...) custom-call(bf16[12,2,64,512]{3,2,1,0:T(8,128)(2,1)} %feat.1, bf16[144,512]{1,0:T(8,128)(2,1)} %w1s.1, ...), custom_call_target="tpu_custom_call" | custom-call | tf_op jit(solution)/shard_map/block/pallas_call | solution.py:903
  242.2 1.3 copy.21
  243.6 1.3 copy.22
  244.9 1.4 copy.29
  246.3 0.0 copy-start.1
  246.3 0.0 copy-start
  246.3 0.0 copy-start.2
  246.3 0.0 copy-start.3
  246.3 4.1 %copy.30 = f32[12,2,64,512]{3,2,1,0:T(8,128)} copy(f32[12,2,64,512]{3,2,1,0:T(8,128)} %get-tuple-element.41) | data formatting | bytes 6291456
  250.4 0.0 copy-done.1
  250.4 0.7 copy.31
  251.1 0.0 copy-done
  251.1 0.7 copy.32
  251.8 0.0 copy-done.2
  251.8 0.6 copy.33
  252.4 0.0 copy-done.3
  252.4 0.5 copy.34
Async XLA Ops:
  246.3 4.1 %copy-start.1 = (f32[144,512]{1,0:T(8,128)S(1)}, f32[144,512]{1,0:T(8,128)}, u32[]{:S(2)}) copy-start(f32[144,512]{1,0:T(8,128)} %get-tuple-element.42) | copy-start | bytes 884740
  246.3 4.8 %copy-start = (f32[144,512]{1,0:T(8,128)S(1)}, f32[144,512]{1,0:T(8,128)}, u32[]{:S(2)}) copy-start(f32[144,512]{1,0:T(8,128)} %get-tuple-element.43) | copy-start | bytes 884740
  246.3 5.5 %copy-start.2 = (f32[16,40]{1,0:T(8,128)S(1)}, f32[16,40]{1,0:T(8,128)}, u32[]{:S(2)}) copy-start(f32[16,40]{1,0:T(8,128)} %get-tuple-element.46) | copy-start | bytes 7684
  246.3 6.1 %copy-start.3 = (f32[1,40]{1,0:T(1,128)S(1)}, f32[1,40]{1,0:T(1,128)}, u32[]{:S(2)}) copy-start(f32[1,40]{1,0:T(1,128)} %get-tuple-element.23) | copy-start | bytes 484
